TPU v7x, 256 devices: a whole 4x4x8 slice. The times are simulated.
256 devices in a mesh: snp: 32 (over y, z), ind: 8 (over x, core).
Axes of the slice: x: 4, y: 4, z: 8, core: 2. Of those that a mesh axis runs over, the one named last changes fastest.
Arguments:
- beta_hat: float32 [64, 32768], P('ind', 'snp'), may hold values from -8 to 8
- ld_band: float32 [32768, 1024], P('snp'), as said below
- band_start: int32 [256], P('snp'), may hold values from -480 to 32224, as said below
- heritability: float32 [64], P('ind'), may hold values from 0.2 to 0.6
- genotypes: bfloat16 [8192, 32768], P('ind', 'snp'), may hold values from 0 to 2, as said below
Outputs:
- weights: float32 [64, 32768], P('ind', 'snp')
- scores: float32 [64, 8192], P(None, ('ind', 'snp'))
Inputs may be any that keep to these rules, and one draw needn't show every extreme that they name: ld_band is a symmetric matrix R in band form: entry k of row i is R[i, band_start[i // 128] + k]; R[i, i] = 1; R[i, j] = 0 when |i - j| > 416 or j lies outside the SNPs; the off-diagonal magnitudes of a row sum to 2.5 at most. `band_start`: block b's window starts at 128 * b - 416 - k with k from 0 to 64; the first block has k = 64 and the last block k = 0. `genotypes`: dosages are 0, 1 or 2.
All inputs are finite; a program needn't handle non-finite values.
Results may differ from a plain program's by a relative error of at most 0.0021.
Values may be sent and summed in bfloat16 or wider, within the bound.
A program may use at most 64 MiB of HBM per device.

v0:
```python
import jax
import jax.numpy as jnp
from jax import lax
from jax.sharding import PartitionSpec as P

BLK = 128
ITERS = 2
M_GENOME = 1100000
N_GWAS = 1000000


def padded_2(block, sides, width):
    for axis, dim in sides:
        count = lax.axis_size(axis)
        forward = [(i, i + 1) for i in range(count - 1)]
        backward = [(target, source) for source, target in forward]
        low = lax.ppermute(
            lax.slice_in_dim(block, block.shape[dim] - width, None, axis=dim), axis, forward
        )
        high = lax.ppermute(lax.slice_in_dim(block, 0, width, axis=dim), axis, backward)
        block = jnp.concatenate([low, block, high], axis=dim)
    return block


def apply_operator(vector, ld_band, band_start, ridge_shift):
    band_cols = ld_band.shape[1]
    halo_cols = band_cols - BLK
    padded = padded_2(vector, (("snp", 1),), halo_cols)
    local_rows = vector.shape[1]
    offsets = band_start - lax.axis_index("snp") * local_rows + halo_cols
    windows = jax.vmap(lambda row_begin: lax.dynamic_slice_in_dim(padded, row_begin, band_cols, 1))(
        offsets
    )
    blocks = ld_band.reshape(band_start.shape[0], BLK, band_cols)
    product = jnp.einsum("btk,brk->tbr", windows, blocks, precision=lax.Precision.HIGHEST)
    return product.reshape(vector.shape) + ridge_shift[:, None] * vector


def norm_sum(residual):
    return lax.psum(jnp.sum(residual * residual, axis=1), "snp")


def local(beta_hat, ld_band, band_start, heritability, genotypes):
    ridge_shift = M_GENOME / N_GWAS / heritability
    weights = jnp.zeros_like(beta_hat)
    residual = beta_hat
    direction = beta_hat
    norm_now = norm_sum(residual)
    for turn_index in range(ITERS):
        product = apply_operator(direction, ld_band, band_start, ridge_shift)
        curved = lax.psum(jnp.sum(direction * product, axis=1), "snp")
        step_size = norm_now / curved
        weights = weights + step_size[:, None] * direction
        residual = residual - step_size[:, None] * product
        if turn_index + 1 < ITERS:
            norm_next = norm_sum(residual)
            direction = residual + (norm_next / norm_now)[:, None] * direction
            norm_now = norm_next
    rounded = weights.astype(jnp.bfloat16)
    partial_scores = lax.dot_general(
        lax.all_gather(rounded, "ind", axis=0, tiled=True),
        genotypes,
        (((1,), (1,)), ((), ())),
        preferred_element_type=jnp.float32,
    )
    complete = lax.psum(partial_scores, "snp")
    count = complete.shape[1] * lax.axis_size("ind")
    summed = lax.psum(jnp.sum(complete, axis=1), "ind")
    average = summed / count
    centred = complete - average[:, None]
    variance = lax.psum(jnp.sum(centred * centred, axis=1), "ind") / count
    share_cols = complete.shape[1] // lax.axis_size("snp")
    own_part = lax.dynamic_slice_in_dim(centred, lax.axis_index("snp") * share_cols, share_cols, 1)
    scores = own_part * lax.rsqrt(variance + 1e-05)[:, None]
    return (weights, scores)


def solution(mesh):
    placed = (P("ind", "snp"), P("snp", None), P("snp"), P("ind"), P("ind", "snp"))
    return jax.shard_map(
        local,
        mesh=mesh,
        in_specs=placed,
        out_specs=(P("ind", "snp"), P(None, ("ind", "snp"))),
        check_vma=False,
    )
```

profile of v0, /device:TPU:1, one launch (start us, length us, event | category | flops | bytes accessed | tf_op | source)
XLA Modules:
  0.0 465.0 jit_solution(3514487914134571717)
XLA Ops:
  7.2 0.9 fusion.7
  8.1 4.4 collective-permute-start
  12.5 1.3 collective-permute-start.1
  15.2 2.2 collective-permute-done.1
  17.3 0.8 pad_maximum_fusion
  18.1 10.5 %while.2 = (s32[]{:T(128)}, f32[8,2816]{1,0:T(8,128)S(1)}, s32[8,2]{0,1:T(2,128)S(1)}, f32[8,8,1024]{2,1,0:T(8,128)S(1)}, s32[]{:T(128)}) while((s32[]{:T(128)}, f32[8,2816]{1,0:T(8,128)S(1)}, s32[8,2]{0,1:T(2,128)S(1)}, f32[8,8,1024]{2,1,0:T(8,128)S(1)}, s32[]{:T(128)}) %tuple.38), condition=%wide.while_cond, body=%wide.while_body.sunk | while | flops 2 | bytes 65633 | solution.py:31
  18.7 0.7 bitcast_dynamic-update-slice_fusion.4
  20.0 0.7 bitcast_dynamic-update-slice_fusion.4
  28.6 5.4 %multiply_reduce_fusion.2 = (f32[8]{0:T(128)S(1)}, f32[8]{0:T(128)S(1)}, f32[8,1024]{1,0:T(8,128)S(1)}) fusion(f32[8,1024]{1,0:T(8,128)} %param.5, f32[8]{0:T(128)S(1)} %broadcast_divide_fusion, f32[8,8,1024]{2,1,0:T(8,128)S(1)} %get-tuple-element.9, f32[8,128,1024]{2,1,0:T(8,128)} %bitcast.39), kind=kOutput, calls=%fused_computation.19 | convolution fusion | flops 100712432 | bytes 4522080 | tf_op jit(solution)/shard_map/btk,brk->tbr/dot_general | solution.py:35
  34.1 62.4 %all-reduce.1 = (f32[8]{0:T(128)S(1)}, f32[8]{0:T(128)S(1)}) all-reduce(f32[8]{0:T(128)S(1)} %get-tuple-element.21, f32[8]{0:T(128)S(1)} %get-tuple-element.20), channel_id=1, replica_groups=mesh['snp'=32,'ind'=8] {'snp'}, use_global_device_ids=true, to_apply=%region_1.0 | all-reduce | flops 16 | bytes 128 | tf_op jit(solution)/shard_map/psum | solution.py:40
  96.6 55.7 %psum.51 = f32[8]{0:T(128)S(1)} all-reduce(f32[8]{0:T(128)S(1)} %multiply_reduce_fusion.1), channel_id=1, replica_groups=mesh['snp'=32,'ind'=8] {'snp'}, use_global_device_ids=true, to_apply=%region_5.0 | all-reduce | flops 8 | bytes 64 | tf_op jit(solution)/shard_map/psum | solution.py:40
  152.5 3.6 collective-permute-start.2
  156.0 1.3 collective-permute-start.3
  157.3 3.6 collective-permute-done.3
  161.0 10.5 %while.3 = (s32[]{:T(128)}, f32[8,2816]{1,0:T(8,128)S(1)}, s32[8,2]{0,1:T(2,128)S(1)}, f32[8,8,1024]{2,1,0:T(8,128)S(1)}, s32[]{:T(128)}) while((s32[]{:T(128)}, f32[8,2816]{1,0:T(8,128)S(1)}, s32[8,2]{0,1:T(2,128)S(1)}, f32[8,8,1024]{2,1,0:T(8,128)S(1)}, s32[]{:T(128)}) %tuple.46), condition=%wide.while_cond.1, body=%wide.while_body.1.sunk | while | flops 2 | bytes 65633 | solution.py:31
  171.5 5.4 %fusion.3 = f32[8]{0:T(128)S(1)} fusion(f32[8,1024]{1,0:T(8,128)S(1)} %multiply_add_fusion.1, f32[8,8,1024]{2,1,0:T(8,128)S(1)} %get-tuple-element.17, f32[8,128,1024]{2,1,0:T(8,128)} %bitcast.40, f32[8]{0:T(128)S(1)} %broadcast_divide_fusion), kind=kOutput, calls=%fused_computation.9 | convolution fusion | flops 100696056 | bytes 4489280 | tf_op jit(solution)/shard_map/btk,brk->tbr/dot_general | solution.py:35
  176.9 55.7 %psum.52 = f32[8]{0:T(128)S(1)} all-reduce(f32[8]{0:T(128)S(1)} %fusion.3), channel_id=1, replica_groups=mesh['snp'=32,'ind'=8] {'snp'}, use_global_device_ids=true, to_apply=%region_7.0 | all-reduce | flops 8 | bytes 64 | tf_op jit(solution)/shard_map/psum | solution.py:51
  233.3 57.2 %all_gather.3 = bf16[64,1024]{1,0:T(8,128)(2,1)S(1)} all-gather(bf16[8,1024]{1,0:T(8,128)(2,1)S(1)} %get-tuple-element.42), channel_id=1, replica_groups=mesh['snp'=32,'ind'=8] {'ind'}, dimensions={0}, use_global_device_ids=true | all-gather | bytes 147456 | tf_op jit(solution)/shard_map/all_gather | solution.py:61
  290.5 1.5 fusion.8
  292.0 133.9 %all-reduce.4.cloned.1.call-done = f32[64,1024]{1,0:T(8,128)} async-done(((f32[64,1024]{1,0:T(8,128)}), f32[64,1024]{1,0:T(8,128)}) %all-reduce.4.cloned.1.call-update) | async-done | bytes 262160 | tf_op jit(solution)/shard_map/psum | solution.py:66
  425.9 1.1 reduce_sum.58
  426.9 16.9 %psum.54 = f32[64]{0:T(128)S(1)} all-reduce(f32[64]{0:T(128)S(1)} %reduce_sum.58), channel_id=1, replica_groups=mesh['snp'=32,'ind'=8] {'ind'}, use_global_device_ids=true, to_apply=%region_10.0 | all-reduce | flops 64 | bytes 512 | tf_op jit(solution)/shard_map/psum | solution.py:68
  443.8 1.1 multiply_reduce_fusion
  445.0 12.4 %psum.55 = f32[64]{0:T(128)S(1)} all-reduce(f32[64]{0:T(128)S(1)} %get-tuple-element.40), channel_id=1, replica_groups=mesh['snp'=32,'ind'=8] {'ind'}, use_global_device_ids=true, to_apply=%region_12.0 | all-reduce | flops 64 | bytes 512 | tf_op jit(solution)/shard_map/psum | solution.py:71
  (71 shorter events, 22.8 us)
Async XLA Ops:
  7.2 283.4 %copy-start = (bf16[1024,1024]{1,0:T(8,128)(2,1)S(1)}, bf16[1024,1024]{1,0:T(8,128)(2,1)}, u32[]{:S(2)}) copy-start(bf16[1024,1024]{1,0:T(8,128)(2,1)} %param.9) | copy-start | bytes 6291460
  7.2 89.3 %copy-start.1 = (f32[8,1024]{1,0:T(8,128)S(1)}, f32[8,1024]{1,0:T(8,128)}, u32[]{:S(2)}) copy-start(f32[8,1024]{1,0:T(8,128)} %param.5) | copy-start | bytes 98308
  7.2 418.7 %all-reduce.4.cloned.1.call-start = ((), (), s32[]{:S(2)}) async-start(), calls=%async_computation | async-start | bytes 524288 | tf_op jit(solution)/shard_map/psum | solution.py:66
  8.1 7.0 %collective-permute-start = (f32[8,896]{1,0:T(8,128)S(1)}, f32[8,896]{1,0:T(8,128)S(1)}, u32[]{:S(2)}, u32[]{:S(2)}) collective-permute-start(f32[8,896]{1,0:T(8,128)S(1)} %get-tuple-element.46), channel_id=1, source_target_pairs={{0,8},{8,16},{16,24},{24,32},{32,40},{40,48},{48,56},{56,64},{64,7... | collective-permute-start | bytes 86024 | tf_op jit(solution)/shard_map/ppermute | solution.py:17
  12.5 4.8 %collective-permute-start.1 = (f32[8,896]{1,0:T(8,128)S(1)}, f32[8,896]{1,0:T(8,128)S(1)}, u32[]{:S(2)}, u32[]{:S(2)}) collective-permute-start(f32[8,896]{1,0:T(8,128)S(1)} %get-tuple-element.47), channel_id=1, source_target_pairs={{8,0},{16,8},{24,16},{32,24},{40,32},{48,40},{56,48},{64,56},{72,6... | collective-permute-start | bytes 86024 | tf_op jit(solution)/shard_map/ppermute | solution.py:20
  152.5 4.9 %collective-permute-start.2 = (f32[8,896]{1,0:T(8,128)S(1)}, f32[8,896]{1,0:T(8,128)S(1)}, u32[]{:S(2)}, u32[]{:S(2)}) collective-permute-start(f32[8,896]{1,0:T(8,128)S(1)} %get-tuple-element.44), channel_id=1, source_target_pairs={{0,8},{8,16},{16,24},{24,32},{32,40},{40,48},{48,56},{56,64},{64,7... | collective-permute-start | bytes 86024 | tf_op jit(solution)/shard_map/ppermute | solution.py:17
  156.0 4.9 %collective-permute-start.3 = (f32[8,896]{1,0:T(8,128)S(1)}, f32[8,896]{1,0:T(8,128)S(1)}, u32[]{:S(2)}, u32[]{:S(2)}) collective-permute-start(f32[8,896]{1,0:T(8,128)S(1)} %get-tuple-element.45), channel_id=1, source_target_pairs={{8,0},{16,8},{24,16},{32,24},{40,32},{48,40},{56,48},{64,56},{72,6... | collective-permute-start | bytes 86024 | tf_op jit(solution)/shard_map/ppermute | solution.py:20
Sparse Core Ops, SparseCore 0:
  292.1 133.6 all-reduce.3
where the time goes:
time: 466 us; the launch traced here: 465 us
  blocking collectives  260 us (56%)
  waiting for transfers between devices  140 us (30%)
  local copies, waits for them, and re-layouts  22.7 us (5%)
  between operations  14.1 us (3%)
  matrix products  12.3 us (3%)
  starting transfers between devices  10.5 us (2%)
  other arithmetic  5.4 us (1%)
    psum x1, waiting for transfers between devices, local(): complete = lax.psum(partial_scores, 'snp')  134 us
    psum x2, blocking collectives, norm_sum(): return lax.psum(jnp.sum(residual * residual, axis=1), 'snp')  118 us
    all_gather x1, blocking collectives, local(): lax.all_gather(rounded, 'ind', axis=0, tiled=True)  57.2 us
    psum x1, blocking collectives, local(): curved = lax.psum(jnp.sum(direction * product, axis=1), 'snp')  55.7 us
    gather x48, local copies, waits for them, and re-layouts  21 us
    psum x1, blocking collectives, local(): summed = lax.psum(jnp.sum(complete, axis=1), 'ind')  16.9 us
    psum x1, blocking collectives, local(): variance = lax.psum(jnp.sum(centred * centred, axis=1), 'ind') / count  12.4 us
    dot_general x2, matrix products, apply_operator(): jnp.einsum('btk,brk->tbr', windows, blocks, precision=lax.Precision.HIGHEST)  10.8 us
  transfers between devices with their start and end apart: 5, of which 3 were waited for; matrix products, arithmetic and copies ran while one was open for 0% of the time, Pallas kernels for 0%

commit v1 on v0

--- a/solution.py
+++ b/solution.py
@@ -63,7 +63,13 @@
         (((1,), (1,)), ((), ())),
         preferred_element_type=jnp.float32,
     )
-    complete = lax.psum(partial_scores, "snp")
+    size = lax.axis_size("snp")
+    complete, far = (partial_scores, 1)
+    while far < size:
+        complete = complete + lax.ppermute(
+            complete, "snp", [(i_2, i_2 ^ far) for i_2 in range(size)]
+        )
+        far = 2 * far
     count = complete.shape[1] * lax.axis_size("ind")
     summed = lax.psum(jnp.sum(complete, axis=1), "ind")
     average = summed / count

time: 466 us -> 365 us (0.78)
  waiting for transfers between devices: 140 us -> 51.1 us
  between operations: 14.1 us -> 0.79 us
    psum x1 -> x0, waiting for transfers between devices: 134 us -> none  [local(): complete = lax.psum(partial_scores, 'snp')]
    ppermute x0 -> x5, waiting for transfers between devices: none -> 45.3 us  [local(): lax.ppermute(complete, 'snp', [(i_2, i_2 ^ far) for i_2 in range(size)])]
  transfers between devices with their start and end apart: 5 -> 9, of which waited for: 3 -> 7; matrix products, arithmetic and copies ran while one was open for 0% -> 0% of each run, Pallas kernels for 0% -> 0%
where the time goes in v1:
time: 365 us; the launch traced here: 364 us
  blocking collectives  262 us (72%)
  waiting for transfers between devices  51.1 us (14%)
  local copies, waits for them, and re-layouts  22.7 us (6%)
  starting transfers between devices  12.7 us (3%)
  matrix products  11.5 us (3%)
    psum x2, blocking collectives, norm_sum(): return lax.psum(jnp.sum(residual * residual, axis=1), 'snp')  118 us
    all_gather x1, blocking collectives, local(): lax.all_gather(rounded, 'ind', axis=0, tiled=True)  57.2 us
    psum x1, blocking collectives, local(): curved = lax.psum(jnp.sum(direction * product, axis=1), 'snp')  55.7 us
    ppermute x5, waiting for transfers between devices, local(): lax.ppermute(complete, 'snp', [(i_2, i_2 ^ far) for i_2 in range(size)])  45.3 us
    gather x48, local copies, waits for them, and re-layouts  21 us
    psum x1, blocking collectives, local(): summed = lax.psum(jnp.sum(complete, axis=1), 'ind')  18.1 us
    psum x1, blocking collectives, local(): variance = lax.psum(jnp.sum(centred * centred, axis=1), 'ind') / count  12.4 us
    dot_general x2, matrix products, apply_operator(): jnp.einsum('btk,brk->tbr', windows, blocks, precision=lax.Precision.HIGHEST)  10.8 us
  transfers between devices with their start and end apart: 9, of which 7 were waited for; matrix products, arithmetic and copies ran while one was open for 0% of the time, Pallas kernels for 0%

profile of v1, /device:TPU:1, one launch (start us, length us, event | category | flops | bytes accessed | tf_op | source)
XLA Modules:
  0.0 364.0 jit_solution(7635444210098882748)
XLA Ops:
  0.7 0.9 fusion.8
  1.6 4.4 %collective-permute-start = (f32[8,896]{1,0:T(8,128)S(1)}, f32[8,896]{1,0:T(8,128)S(1)}, u32[]{:S(2)}, u32[]{:S(2)}) collective-permute-start(f32[8,896]{1,0:T(8,128)S(1)} %get-tuple-element.48), channel_id=1, source_target_pairs={{0,8},{8,16},{16,24},{24,32},{32,40},{40,48},{48,56},{56,64},{64,7... | collective-permute-start | bytes 86024 | tf_op jit(solution)/shard_map/ppermute | solution.py:17
  5.9 1.3 collective-permute-start.1
  8.6 2.2 collective-permute-done.1
  10.7 0.8 pad_maximum_fusion
  11.5 10.5 %while.2 = (s32[]{:T(128)}, f32[8,2816]{1,0:T(8,128)S(1)}, s32[8,2]{0,1:T(2,128)S(1)}, f32[8,8,1024]{2,1,0:T(8,128)S(1)}, s32[]{:T(128)}) while((s32[]{:T(128)}, f32[8,2816]{1,0:T(8,128)S(1)}, s32[8,2]{0,1:T(2,128)S(1)}, f32[8,8,1024]{2,1,0:T(8,128)S(1)}, s32[]{:T(128)}) %tuple.39), condition=%wide.while_cond, body=%wide.while_body.sunk | while | flops 2 | bytes 65641 | solution.py:31
  22.1 5.4 %multiply_reduce_fusion.2 = (f32[8]{0:T(128)S(1)}, f32[8]{0:T(128)S(1)}, f32[8,1024]{1,0:T(8,128)S(1)}) fusion(f32[8,1024]{1,0:T(8,128)} %param.5, f32[8]{0:T(128)S(1)} %broadcast_divide_fusion, f32[8,8,1024]{2,1,0:T(8,128)S(1)} %get-tuple-element.9, f32[8,128,1024]{2,1,0:T(8,128)} %bitcast.39), kind=kOutput, calls=%fused_computation.19 | convolution fusion | flops 100712432 | bytes 4522080 | tf_op jit(solution)/shard_map/btk,brk->tbr/dot_general | solution.py:35
  27.5 62.4 %all-reduce.1 = (f32[8]{0:T(128)S(1)}, f32[8]{0:T(128)S(1)}) all-reduce(f32[8]{0:T(128)S(1)} %get-tuple-element.21, f32[8]{0:T(128)S(1)} %get-tuple-element.20), channel_id=1, replica_groups=mesh['snp'=32,'ind'=8] {'snp'}, use_global_device_ids=true, to_apply=%region_1.0 | all-reduce | flops 16 | bytes 128 | tf_op jit(solution)/shard_map/psum | solution.py:40
  90.1 55.7 %psum.44 = f32[8]{0:T(128)S(1)} all-reduce(f32[8]{0:T(128)S(1)} %multiply_reduce_fusion.1), channel_id=1, replica_groups=mesh['snp'=32,'ind'=8] {'snp'}, use_global_device_ids=true, to_apply=%region_5.0 | all-reduce | flops 8 | bytes 64 | tf_op jit(solution)/shard_map/psum | solution.py:40
  145.9 3.6 collective-permute-start.2
  149.5 1.3 collective-permute-start.3
  150.8 3.6 collective-permute-done.3
  154.4 10.5 %while.3 = (s32[]{:T(128)}, f32[8,2816]{1,0:T(8,128)S(1)}, s32[8,2]{0,1:T(2,128)S(1)}, f32[8,8,1024]{2,1,0:T(8,128)S(1)}, s32[]{:T(128)}) while((s32[]{:T(128)}, f32[8,2816]{1,0:T(8,128)S(1)}, s32[8,2]{0,1:T(2,128)S(1)}, f32[8,8,1024]{2,1,0:T(8,128)S(1)}, s32[]{:T(128)}) %tuple.45), condition=%wide.while_cond.1, body=%wide.while_body.1.sunk | while | flops 2 | bytes 65641 | solution.py:31
  164.9 5.4 %fusion.3 = f32[8]{0:T(128)S(1)} fusion(f32[8,1024]{1,0:T(8,128)S(1)} %multiply_add_fusion.1, f32[8,8,1024]{2,1,0:T(8,128)S(1)} %get-tuple-element.17, f32[8,128,1024]{2,1,0:T(8,128)} %bitcast.40, f32[8]{0:T(128)S(1)} %broadcast_divide_fusion), kind=kOutput, calls=%fused_computation.9 | convolution fusion | flops 100696056 | bytes 4489280 | tf_op jit(solution)/shard_map/btk,brk->tbr/dot_general | solution.py:35
  170.3 55.7 %psum.45 = f32[8]{0:T(128)S(1)} all-reduce(f32[8]{0:T(128)S(1)} %fusion.3), channel_id=1, replica_groups=mesh['snp'=32,'ind'=8] {'snp'}, use_global_device_ids=true, to_apply=%region_7.0 | all-reduce | flops 8 | bytes 64 | tf_op jit(solution)/shard_map/psum | solution.py:51
  226.7 57.2 %all_gather.3 = bf16[64,1024]{1,0:T(8,128)(2,1)S(1)} all-gather(bf16[8,1024]{1,0:T(8,128)(2,1)S(1)} %get-tuple-element.44), channel_id=1, replica_groups=mesh['snp'=32,'ind'=8] {'ind'}, dimensions={0}, use_global_device_ids=true | all-gather | bytes 147456 | tf_op jit(solution)/shard_map/all_gather | solution.py:61
  284.7 1.8 collective-permute-start.4
  286.5 6.6 %collective-permute-done.4 = f32[64,1024]{1,0:T(8,128)S(1)} collective-permute-done((f32[64,1024]{1,0:T(8,128)S(1)}, f32[64,1024]{1,0:T(8,128)S(1)}, u32[]{:S(2)}, u32[]{:S(2)}) %collective-permute-start.4) | collective-permute-done | bytes 262176 | tf_op jit(solution)/shard_map/ppermute | solution.py:69
  293.2 13.8 %collective-permute-done.5 = f32[64,1024]{1,0:T(8,128)S(1)} collective-permute-done((f32[64,1024]{1,0:T(8,128)S(1)}, f32[64,1024]{1,0:T(8,128)S(1)}, u32[]{:S(2)}, u32[]{:S(2)}) %collective-permute-start.5) | collective-permute-done | bytes 262176 | tf_op jit(solution)/shard_map/ppermute | solution.py:69
  307.2 13.0 %collective-permute-done.6 = f32[64,1024]{1,0:T(8,128)S(1)} collective-permute-done((f32[64,1024]{1,0:T(8,128)S(1)}, f32[64,1024]{1,0:T(8,128)S(1)}, u32[]{:S(2)}, u32[]{:S(2)}) %collective-permute-start.6) | collective-permute-done | bytes 262176 | tf_op jit(solution)/shard_map/ppermute | solution.py:69
  320.3 5.2 %collective-permute-done.7 = f32[64,1024]{1,0:T(8,128)S(1)} collective-permute-done((f32[64,1024]{1,0:T(8,128)S(1)}, f32[64,1024]{1,0:T(8,128)S(1)}, u32[]{:S(2)}, u32[]{:S(2)}) %collective-permute-start.7) | collective-permute-done | bytes 262176 | tf_op jit(solution)/shard_map/ppermute | solution.py:69
  325.7 6.7 %collective-permute-done.8 = f32[64,1024]{1,0:T(8,128)S(1)} collective-permute-done((f32[64,1024]{1,0:T(8,128)S(1)}, f32[64,1024]{1,0:T(8,128)S(1)}, u32[]{:S(2)}, u32[]{:S(2)}) %collective-permute-start.8) | collective-permute-done | bytes 262176 | tf_op jit(solution)/shard_map/ppermute | solution.py:69
  332.5 18.1 %psum.46 = f32[64]{0:T(128)S(1)} all-reduce(f32[64]{0:T(128)S(1)} %get-tuple-element.42), channel_id=1, replica_groups=mesh['snp'=32,'ind'=8] {'ind'}, use_global_device_ids=true, to_apply=%region_9.0 | all-reduce | flops 64 | bytes 512 | tf_op jit(solution)/shard_map/psum | solution.py:74
  350.8 12.4 %psum.47 = f32[64]{0:T(128)S(1)} all-reduce(f32[64]{0:T(128)S(1)} %get-tuple-element.40), channel_id=1, replica_groups=mesh['snp'=32,'ind'=8] {'ind'}, use_global_device_ids=true, to_apply=%region_11.0 | all-reduce | flops 64 | bytes 512 | tf_op jit(solution)/shard_map/psum | solution.py:77
  (82 shorter events, 25.8 us)
Async XLA Ops:
  0.6 283.3 %copy-start = (bf16[1024,1024]{1,0:T(8,128)(2,1)S(1)}, bf16[1024,1024]{1,0:T(8,128)(2,1)}, u32[]{:S(2)}) copy-start(bf16[1024,1024]{1,0:T(8,128)(2,1)} %param.9) | copy-start | bytes 6291460
  0.6 89.2 %copy-start.1 = (f32[8,1024]{1,0:T(8,128)S(1)}, f32[8,1024]{1,0:T(8,128)}, u32[]{:S(2)}) copy-start(f32[8,1024]{1,0:T(8,128)} %param.5) | copy-start | bytes 98308
  1.6 7.0 %collective-permute-start = (f32[8,896]{1,0:T(8,128)S(1)}, f32[8,896]{1,0:T(8,128)S(1)}, u32[]{:S(2)}, u32[]{:S(2)}) collective-permute-start(f32[8,896]{1,0:T(8,128)S(1)} %get-tuple-element.48), channel_id=1, source_target_pairs={{0,8},{8,16},{16,24},{24,32},{32,40},{40,48},{48,56},{56,64},{64,7... | collective-permute-start | bytes 86024 | tf_op jit(solution)/shard_map/ppermute | solution.py:17
  5.9 4.8 %collective-permute-start.1 = (f32[8,896]{1,0:T(8,128)S(1)}, f32[8,896]{1,0:T(8,128)S(1)}, u32[]{:S(2)}, u32[]{:S(2)}) collective-permute-start(f32[8,896]{1,0:T(8,128)S(1)} %get-tuple-element.49), channel_id=1, source_target_pairs={{8,0},{16,8},{24,16},{32,24},{40,32},{48,40},{56,48},{64,56},{72,6... | collective-permute-start | bytes 86024 | tf_op jit(solution)/shard_map/ppermute | solution.py:20
  145.9 4.9 %collective-permute-start.2 = (f32[8,896]{1,0:T(8,128)S(1)}, f32[8,896]{1,0:T(8,128)S(1)}, u32[]{:S(2)}, u32[]{:S(2)}) collective-permute-start(f32[8,896]{1,0:T(8,128)S(1)} %get-tuple-element.46), channel_id=1, source_target_pairs={{0,8},{8,16},{16,24},{24,32},{32,40},{40,48},{48,56},{56,64},{64,7... | collective-permute-start | bytes 86024 | tf_op jit(solution)/shard_map/ppermute | solution.py:17
  149.5 4.9 %collective-permute-start.3 = (f32[8,896]{1,0:T(8,128)S(1)}, f32[8,896]{1,0:T(8,128)S(1)}, u32[]{:S(2)}, u32[]{:S(2)}) collective-permute-start(f32[8,896]{1,0:T(8,128)S(1)} %get-tuple-element.47), channel_id=1, source_target_pairs={{8,0},{16,8},{24,16},{32,24},{40,32},{48,40},{56,48},{64,56},{72,6... | collective-permute-start | bytes 86024 | tf_op jit(solution)/shard_map/ppermute | solution.py:20
  284.7 8.4 %collective-permute-start.4 = (f32[64,1024]{1,0:T(8,128)S(1)}, f32[64,1024]{1,0:T(8,128)S(1)}, u32[]{:S(2)}, u32[]{:S(2)}) collective-permute-start(f32[64,1024]{1,0:T(8,128)S(1)} %fusion.9), channel_id=1, source_target_pairs={{0,8},{8,0},{16,24},{24,16},{32,40},{40,32},{48,56},{56,48},{64,72... | collective-permute-start | bytes 786440 | tf_op jit(solution)/shard_map/ppermute | solution.py:69
  293.1 13.9 %collective-permute-start.5 = (f32[64,1024]{1,0:T(8,128)S(1)}, f32[64,1024]{1,0:T(8,128)S(1)}, u32[]{:S(2)}, u32[]{:S(2)}) collective-permute-start(f32[64,1024]{1,0:T(8,128)S(1)} %add.69), channel_id=1, source_target_pairs={{0,16},{8,24},{16,0},{24,8},{32,48},{40,56},{48,32},{56,40},{64,80... | collective-permute-start | bytes 786440 | tf_op jit(solution)/shard_map/ppermute | solution.py:69
  307.1 13.1 %collective-permute-start.6 = (f32[64,1024]{1,0:T(8,128)S(1)}, f32[64,1024]{1,0:T(8,128)S(1)}, u32[]{:S(2)}, u32[]{:S(2)}) collective-permute-start(f32[64,1024]{1,0:T(8,128)S(1)} %add.70), channel_id=1, source_target_pairs={{0,32},{8,40},{16,48},{24,56},{32,0},{40,8},{48,16},{56,24},{64,96... | collective-permute-start | bytes 786440 | tf_op jit(solution)/shard_map/ppermute | solution.py:69
  320.2 5.3 %collective-permute-start.7 = (f32[64,1024]{1,0:T(8,128)S(1)}, f32[64,1024]{1,0:T(8,128)S(1)}, u32[]{:S(2)}, u32[]{:S(2)}) collective-permute-start(f32[64,1024]{1,0:T(8,128)S(1)} %add.71), channel_id=1, source_target_pairs={{0,64},{8,72},{16,80},{24,88},{32,96},{40,104},{48,112},{56,120},{... | collective-permute-start | bytes 786440 | tf_op jit(solution)/shard_map/ppermute | solution.py:69
  325.6 6.8 %collective-permute-start.8 = (f32[64,1024]{1,0:T(8,128)S(1)}, f32[64,1024]{1,0:T(8,128)S(1)}, u32[]{:S(2)}, u32[]{:S(2)}) collective-permute-start(f32[64,1024]{1,0:T(8,128)S(1)} %add.72), channel_id=1, source_target_pairs={{0,128},{8,136},{16,144},{24,152},{32,160},{40,168},{48,176},{56,1... | collective-permute-start | bytes 786440 | tf_op jit(solution)/shard_map/ppermute | solution.py:69
